TPU v7x, 256 devices: a whole 4x4x8 slice. The times are simulated.
256 devices in a mesh: section: 4 (over y_lo, core), dp: 4 (over x), expert: 16 (over z, y_hi).
Axes of the slice: x: 4, y: 4 (y_hi: 2, y_lo: 2; y = y_hi * 2 + y_lo), z: 8, core: 2. Of those that a mesh axis runs over, the one named last changes fastest.
Arguments:
- inbound: bfloat16 [32768, 2048], P(('section', 'dp', 'expert')), may hold values from -6 to 6
- expert_ids: int32 [32768, 1], P(('section', 'dp', 'expert')), may hold values from 0 to 3
- gates: float32 [32768, 1], P(('section', 'dp', 'expert')), may hold values from 0.2 to 1
- w_in: bfloat16 [4, 2048, 8192], P('section', None, 'expert'), may hold values from -0.125 to 0.125
- w_out: bfloat16 [4, 8192, 2048], P('section', 'expert'), may hold values from -0.0625 to 0.0625
- mlp_in: bfloat16 [2048, 8192], P(None, 'expert'), may hold values from -0.125 to 0.125
- mlp_out: bfloat16 [8192, 2048], P('expert'), may hold values from -0.0625 to 0.0625
Outputs:
- mixed: bfloat16 [32768, 2048], P(('section', 'dp', 'expert'))
All inputs are finite; a program needn't handle non-finite values.
Results may differ from a plain program's by a relative error of at most 0.02.
Values may be sent and summed in bfloat16 or wider, within the bound.
A program may use at most 128 MiB of HBM per device.

v0:
```python
import jax
import jax.numpy as jnp
from jax import lax
from jax.sharding import PartitionSpec as P


def passed_along(block, axis, distance):
    devices = range(lax.axis_size(axis))
    route = [((i - distance) % len(devices), i) for i in devices]
    return lax.ppermute(block, axis, route)


def activate(rows, weights):
    return jax.nn.gelu(
        jnp.dot(rows, weights, preferred_element_type=jnp.float32), approximate=True
    ).astype(jnp.bfloat16)


def shards(inbound, expert_ids, gates, w_in, w_out, mlp_in, mlp_out):
    tokens = passed_along(inbound, "section", 1)
    width_model = tokens.shape[1]
    own_rows = tokens.shape[0]
    experts = w_in.shape[0] * lax.axis_size("section")
    capacity = own_rows * 5 // 32
    chosen = expert_ids[:, 0]
    labels = jnp.arange(experts, dtype=jnp.int32)
    onehot = (chosen[:, None] == labels[None, :]).astype(jnp.int32)
    before = jnp.cumsum(onehot, axis=0) - onehot
    position = jnp.sum(before * onehot, axis=1)
    slots = jnp.arange(capacity, dtype=jnp.int32)
    placing = (
        (chosen[None, None, :] == labels[:, None, None])
        & (position[None, None, :] == slots[None, :, None])
    ).astype(jnp.bfloat16)
    outbound = jnp.einsum(
        "ect,td->ecd", placing, tokens, preferred_element_type=jnp.float32
    ).astype(jnp.bfloat16)
    arrived = lax.all_to_all(outbound, "section", split_axis=0, concat_axis=0, tiled=True)
    expert_rows = arrived.reshape(-1, width_model)
    weight_in = w_in[0]
    weight_out = w_out[0]
    dense_hidden = activate(lax.all_gather(tokens, "expert", axis=0, tiled=True), mlp_in)
    dense_out = lax.psum_scatter(
        jnp.dot(dense_hidden, mlp_out, preferred_element_type=jnp.float32).astype(jnp.bfloat16),
        "expert",
        scatter_dimension=0,
        tiled=True,
    ).astype(jnp.float32)
    expert_hidden = activate(lax.all_gather(expert_rows, "expert", axis=0, tiled=True), weight_in)
    expert_sum = lax.psum_scatter(
        jnp.dot(expert_hidden, weight_out, preferred_element_type=jnp.float32).astype(jnp.bfloat16),
        "expert",
        scatter_dimension=0,
        tiled=True,
    )
    leaving = expert_sum.reshape(-1, capacity, width_model)
    returned_rows = lax.all_to_all(leaving, "section", split_axis=0, concat_axis=0, tiled=True)
    expert_part = jnp.einsum(
        "ect,ecd->td", placing, returned_rows, preferred_element_type=jnp.float32
    )
    return (dense_out + gates * expert_part).astype(jnp.bfloat16)


def solution(mesh):
    return jax.shard_map(
        shards,
        mesh=mesh,
        in_specs=(
            P(("section", "dp", "expert"), None),
            P(("section", "dp", "expert"), None),
            P(("section", "dp", "expert"), None),
            P("section", None, "expert"),
            P("section", "expert", None),
            P(None, "expert"),
            P("expert", None),
        ),
        out_specs=P(("section", "dp", "expert"), None),
        check_vma=False,
    )
```

profile of v0, /device:TPU:1, one launch (start us, length us, event | category | flops | bytes accessed | tf_op | source)
XLA Modules:
  0.0 720.6 jit_solution(4078446821017907553)
XLA Ops:
  6.5 0.0 copy-start
  6.5 0.0 all-gather.5.cloned.1.call-start
  6.5 2.7 collective-permute-start
  9.2 0.7 fusion.32
  10.0 0.2 reduce_window_sum.11
  10.1 0.8 select_reduce_fusion
  11.0 0.7 iota_compare_fusion.2
  11.7 4.0 collective-permute-done
  15.7 0.0 copy-start.1
  15.7 0.3 convolution_convert_fusion.2
  15.9 11.7 %all_to_all.10 = bf16[4,20,2048]{2,1,0:T(8,128)(2,1)S(1)} all-to-all(bf16[4,20,2048]{2,1,0:T(8,128)(2,1)S(1)} %convolution_convert_fusion.2), channel_id=1, replica_groups=mesh['section'=4,'dp'=4,'expert'=16] {'section'}, dimensions={0} | all-to-all | bytes 655360 | tf_op jit(solution)/shard_map/all_to_all | solution.py:38
  27.7 0.8 reshape.55
  28.5 0.0 all-gather.5.cloned.1.call-update
  28.5 0.0 all-gather.3.cloned.1.call-start
  28.5 0.0 copy-done.1
  28.5 0.7 all-gather.3.cloned.1.call-update
  29.2 0.0 reduce-scatter.5.cloned.1.call-start
  29.3 105.9 %all-gather.5.cloned.1.call-done = bf16[1280,2048]{1,0:T(8,128)(2,1)} async-done(((bf16[80,2048]{1,0:T(8,128)(2,1)}), bf16[1280,2048]{1,0:T(8,128)(2,1)}) %all-gather.5.cloned.1.call-update) | async-done | bytes 5242896 | tf_op jit(solution)/shard_map/all_gather | solution.py:49
  135.1 10.8 %convolution_convert_fusion = bf16[1280,2048]{1,0:T(8,128)(2,1)} fusion(bf16[1,512,2048]{2,1,0:T(8,128)(2,1)} %param.11, bf16[1280,2048]{1,0:T(8,128)(2,1)} %all-gather.5.cloned.1.call-done, bf16[1,2048,512]{2,1,0:T(8,128)(2,1)} %param.10), kind=kOutput, calls=%fused_computation | convolution fusion | flops 5377228800 | bytes 14680064 | tf_op jit(solution)/shard_map/dot_general | solution.py:51
  145.9 0.0 reduce-scatter.5.cloned.1.call-update
  145.9 0.0 reduce-scatter.3.cloned.1.call-start
  146.0 126.6 %all-gather.3.cloned.1.call-done = bf16[2048,2048]{1,0:T(8,128)(2,1)} async-done(((bf16[128,2048]{1,0:T(8,128)(2,1)}), bf16[2048,2048]{1,0:T(8,128)(2,1)}) %all-gather.3.cloned.1.call-update) | async-done | bytes 8388624 | tf_op jit(solution)/shard_map/all_gather | solution.py:42
  272.6 0.0 copy-done
  272.6 14.4 %convolution_convert_fusion.1 = bf16[2048,2048]{1,0:T(8,128)(2,1)} fusion(bf16[512,2048]{1,0:T(8,128)(2,1)S(1)} %copy-done, bf16[2048,2048]{1,0:T(8,128)(2,1)} %all-gather.3.cloned.1.call-done, bf16[2048,512]{1,0:T(8,128)(2,1)} %param.12), kind=kOutput, calls=%fused_computation.1 | convolution fusion | flops 8603566080 | bytes 20971520 | tf_op jit(solution)/shard_map/dot_general | solution.py:44
  287.0 0.0 copy-start.2
  287.0 0.0 reduce-scatter.3.cloned.1.call-update
  287.0 199.4 %reduce-scatter.5.cloned.1.call-done = bf16[80,2048]{1,0:T(8,128)(2,1)} async-done(((bf16[1280,2048]{1,0:T(8,128)(2,1)}), bf16[80,2048]{1,0:T(8,128)(2,1)}) %reduce-scatter.5.cloned.1.call-update) | async-done | bytes 327696 | tf_op jit(solution)/shard_map/reduce_scatter | solution.py:50
  486.5 1.0 reshape.56
  487.5 13.4 %all_to_all.11 = bf16[4,20,2048]{2,1,0:T(8,128)(2,1)S(1)} all-to-all(bf16[4,20,2048]{2,1,0:T(8,128)(2,1)S(1)} %reshape.56), channel_id=1, replica_groups=mesh['section'=4,'dp'=4,'expert'=16] {'section'}, dimensions={0} | all-to-all | bytes 655360 | tf_op jit(solution)/shard_map/all_to_all | solution.py:57
  500.9 211.0 %reduce-scatter.3.cloned.1.call-done = bf16[128,2048]{1,0:T(8,128)(2,1)} async-done(((bf16[2048,2048]{1,0:T(8,128)(2,1)}), bf16[128,2048]{1,0:T(8,128)(2,1)}) %reduce-scatter.3.cloned.1.call-update) | async-done | bytes 524304 | tf_op jit(solution)/shard_map/reduce_scatter | solution.py:43
  711.9 0.0 copy-done.2
  711.9 2.2 fusion.18
  (1 shorter events, 0.0 us)
Async XLA Ops:
  6.5 266.1 %copy-start = (bf16[512,2048]{1,0:T(8,128)(2,1)S(1)}, bf16[512,2048]{1,0:T(8,128)(2,1)}, u32[]{:S(2)}) copy-start(bf16[512,2048]{1,0:T(8,128)(2,1)} %param.13) | copy-start | bytes 6291460
  6.5 128.6 %all-gather.5.cloned.1.call-start = ((), (), s32[]{:S(2)}) async-start(), calls=%async_computation.6 | async-start | bytes 5570560 | tf_op jit(solution)/shard_map/all_gather | solution.py:49
  6.5 9.1 %collective-permute-start = (bf16[128,2048]{1,0:T(8,128)(2,1)}, bf16[128,2048]{1,0:T(8,128)(2,1)S(1)}, u32[]{:S(2)}, u32[]{:S(2)}) collective-permute-start(bf16[128,2048]{1,0:T(8,128)(2,1)} %param.7), channel_id=1, source_target_pairs={{192,0},{0,64},{64,128},{128,192},{193,1},{1,65},{65,129},{129,193... | collective-permute-start | bytes 1572872 | tf_op jit(solution)/shard_map/ppermute | solution.py:10
  15.7 12.9 %copy-start.1 = (bf16[128,2048]{1,0:T(8,128)(2,1)}, bf16[128,2048]{1,0:T(8,128)(2,1)S(1)}, u32[]{:S(2)}) copy-start(bf16[128,2048]{1,0:T(8,128)(2,1)S(1)} %collective-permute-done) | copy-start | bytes 1572868
  28.5 244.1 %all-gather.3.cloned.1.call-start = ((), (), s32[]{:S(2)}) async-start(), calls=%async_computation.4 | async-start | bytes 8912896 | tf_op jit(solution)/shard_map/all_gather | solution.py:42
  29.2 457.3 %reduce-scatter.5.cloned.1.call-start = ((), (), s32[]{:S(2)}) async-start(), calls=%async_computation.7 | async-start | bytes 5570560 | tf_op jit(solution)/shard_map/reduce_scatter | solution.py:50
  145.9 566.0 %reduce-scatter.3.cloned.1.call-start = ((), (), s32[]{:S(2)}) async-start(), calls=%async_computation.5 | async-start | bytes 8912896 | tf_op jit(solution)/shard_map/reduce_scatter | solution.py:43
  287.0 424.9 %copy-start.2 = (f32[128,1]{0,1:T(1,128)S(1)}, f32[128,1]{0,1:T(1,128)}, u32[]{:S(2)}) copy-start(f32[128,1]{0,1:T(1,128)} %param.9) | copy-start | bytes 1540
Sparse Core Ops, SparseCore 0:
  28.6 106.4 all-gather.4
  137.7 134.8 all-gather.2
  276.7 209.7 reduce-scatter.4
  491.0 220.8 reduce-scatter.2
where the time goes:
time: 724 us; the launch traced here: 721 us
  waiting for transfers between devices  648 us (90%)
  matrix products  27.6 us (4%)
  blocking collectives  25.1 us (3%)
  between operations  13.2 us (2%)
    reduce_scatter x1, waiting for transfers between devices, shards(): lax.psum_scatter(jnp.dot(dense_hidden, mlp_out, preferred_element_type=jn...  211 us
    reduce_scatter x1, waiting for transfers between devices, shards(): lax.psum_scatter(jnp.dot(expert_hidden, weight_out, preferred_element_typ...  199 us
    all_gather x1, waiting for transfers between devices, shards(): lax.all_gather(tokens, 'expert', axis=0, tiled=True)  127 us
    all_gather x1, waiting for transfers between devices, shards(): lax.all_gather(expert_rows, 'expert', axis=0, tiled=True)  106 us
  transfers between devices with their start and end apart: 5, of which 5 were waited for; matrix products, arithmetic and copies ran while one was open for 4% of the time, Pallas kernels for 0%

commit v1 on v0

v1 whole, which is shorter than its diff:
```python
import functools

import jax
import jax.numpy as jnp
from jax import lax
from jax.experimental import pallas as pl
from jax.experimental.pallas import tpu as pltpu
from jax.sharding import PartitionSpec as P

MESH = pl.DeviceIdType.MESH
F32 = jnp.float32
BF16 = jnp.bfloat16
ROWS = 128
HALF = 64
CAP = 20
SLOT = 48
COLS = 256


def relayed_experts(
    ids_ref, gates_ref, inbound, w_in, w_out, mlp_in, mlp_out, out_ref,
    own_in, own_out, far_in, far_out, eown_in, eown_out, efar_in, efar_out,
    x, info, picked, rows, hid, ehid, dense, leaving, back, rs_out, rs_in,
    local_sem, hand_s, hand_r, info_s, info_r, ag_s, ag_r, w1_s, w1_r, w2_s, w2_r,
    core_s, core_r, disp_s, disp_r, ret_s, ret_r, rs_s, rs_r,
):
    s, d, e = lax.axis_index("section"), lax.axis_index("dp"), lax.axis_index("expert")
    core = lax.rem(s, 2)
    flip_e = e + 1 - 2 * lax.rem(e, 2)

    def along_z(k):
        return (s, d, lax.rem(e + 2 * (k % 8), 16))

    def at_section(k):
        return (lax.rem(s + k % 4, 4), d, e)

    def along_x(k):
        return (s, lax.rem(d + k % 4, 4), e)

    other_core = (s + 1 - 2 * core, d, e)
    far_expert = (s, d, flip_e)
    far_mlp = (lax.rem(s + 2, 4), d, flip_e)

    barrier = pltpu.get_barrier_semaphore()
    partners = [along_z(k) for k in range(1, 8)] + [at_section(k) for k in (1, 2, 3)]
    partners += [along_x(1), along_x(3), far_expert, far_mlp]
    for partner in partners:
        pl.semaphore_signal(barrier, inc=1, device_id=partner, device_id_type=MESH)

    local = [
        pltpu.make_async_copy(src, dst, local_sem.at[i])
        for i, (src, dst) in enumerate(
            [(mlp_in, own_in), (mlp_out, own_out), (w_in, eown_in), (w_out, eown_out)]
        )
    ]
    for copy in local:
        copy.start()
    pl.semaphore_wait(barrier, len(partners))

    sent = []

    def send(src, dst, send_sem, recv_sem, device):
        copy = pltpu.make_async_remote_copy(
            src_ref=src, dst_ref=dst, send_sem=send_sem, recv_sem=recv_sem,
            device_id=device, device_id_type=MESH,
        )
        copy.start()
        sent.append(copy)

    def arrived(dst, send_sem, recv_sem, device):
        pltpu.make_async_remote_copy(
            src_ref=dst, dst_ref=dst, send_sem=send_sem, recv_sem=recv_sem,
            device_id=device, device_id_type=MESH,
        ).wait_recv()

    for c in range(2):
        part = pl.ds(c * HALF, HALF)
        send(inbound.at[part], x.at[3, part], hand_s.at[c], hand_r.at[c], at_section(1))

    streams = [
        (mlp_in, far_in, 256, core * 1024, far_mlp),
        (mlp_out, far_out, 64, core * 256, far_mlp),
        (w_in, efar_in, 512, 0, far_expert),
        (w_out, efar_out, 128, 0, far_expert),
    ]

    def quarter(i, ref, k, part=None):
        _, _, q, base, _ = streams[i]
        first = base + lax.rem(d + k % 4, 4) * q
        if part is None:
            return ref.at[pl.ds(pl.multiple_of(first, 64), q)]
        return ref.at[pl.ds(pl.multiple_of(first + part * (q // 2), 32), q // 2)]

    def leg1(i):
        src, dst, _, _, device = streams[i]
        send(quarter(i, src, 0), quarter(i, dst, 0), w1_s.at[i], w1_r.at[i], device)

    def leg2(i):
        dst, device = streams[i][1], streams[i][4]
        mine = quarter(i, dst, 0)
        arrived(mine, w1_s.at[i], w1_r.at[i], device)
        send(mine, mine, w2_s.at[i, 0], w2_r.at[i, 0], along_x(1))
        send(mine, mine, w2_s.at[i, 1], w2_r.at[i, 1], along_x(3))

    def leg3(i):
        dst = streams[i][1]
        arrived(quarter(i, dst, 3), w2_s.at[i, 0], w2_r.at[i, 0], along_x(3))
        part = quarter(i, dst, 3, 0)
        send(part, part, w2_s.at[i, 2], w2_r.at[i, 2], along_x(1))
        arrived(quarter(i, dst, 1), w2_s.at[i, 1], w2_r.at[i, 1], along_x(1))
        part = quarter(i, dst, 1, 1)
        send(part, part, w2_s.at[i, 3], w2_r.at[i, 3], along_x(3))

    def leg4(i):
        dst = streams[i][1]
        arrived(quarter(i, dst, 2, 0), w2_s.at[i, 2], w2_r.at[i, 2], along_x(3))
        arrived(quarter(i, dst, 2, 1), w2_s.at[i, 3], w2_r.at[i, 3], along_x(1))

    def mlp_half(i, side):
        dst = streams[i][1]
        n = streams[i][2] * 4
        return dst.at[pl.ds(pl.multiple_of(side * n, 64), n)]

    leg1(0)
    leg1(1)
    leg1(2)

    ids = jnp.broadcast_to(ids_ref[...].astype(F32), (ROWS, ROWS))
    earlier = lax.broadcasted_iota(jnp.int32, (ROWS, ROWS), 0)
    token = lax.broadcasted_iota(jnp.int32, (ROWS, ROWS), 1)
    same = jnp.where((ids.T == ids) & (earlier < token), 1.0, 0.0)
    position = jnp.sum(same, axis=0, keepdims=True)
    relative = ids_ref[...] - s
    relative = jnp.where(relative < 0, relative + 4, relative).astype(F32)
    code = jnp.where(position < CAP, relative * SLOT + position, -1000.0)
    line = lax.broadcasted_iota(jnp.int32, (8, ROWS), 0)
    info[0] = jnp.where(
        line == 0,
        jnp.broadcast_to(code, (8, ROWS)),
        jnp.broadcast_to(gates_ref[...], (8, ROWS)),
    )
    for k in range(1, 8):
        send(info.at[0], info.at[k], info_s.at[k], info_r.at[k], along_z(k))

    step = (1, -1)

    def place(direction, hop, c):
        if hop == 4:
            return x.at[3, pl.ds(ROWS + c * HALF, HALF)]
        return x.at[hop - 1, pl.ds(direction * ROWS + c * HALF, HALF)]

    def chunks(direction):
        return (0, 1) if direction == 0 else (1, 0)

    def hop_out(direction, hop, c, src):
        send(
            src, place(direction, hop, c),
            ag_s.at[direction, hop - 1, c], ag_r.at[direction, hop - 1, c],
            along_z(step[direction]),
        )

    def hop_in(hop):
        for i in range(2 if hop < 4 else 1):
            for direction in range(2):
                c = chunks(direction)[i]
                dst = place(direction, hop, c)
                arrived(
                    dst, ag_s.at[direction, hop - 1, c], ag_r.at[direction, hop - 1, c],
                    along_z(-step[direction]),
                )
                if hop < 3 or (hop == 3 and i == 0):
                    hop_out(direction, hop + 1, c, dst)

    for c in range(2):
        own = x.at[3, pl.ds(c * HALF, HALF)]
        arrived(own, hand_s.at[c], hand_r.at[c], at_section(3))
        for direction in range(2):
            hop_out(direction, 1, c, own)
    leg1(3)

    sources = [(1, 7), (2, 6), (3, 5), (0, 4)]

    def placing(g, weighted):
        parts = []
        for side, k in enumerate(sources[g]):
            slot = lax.broadcasted_iota(jnp.int32, (4 * SLOT, ROWS), 0).astype(F32)
            want = info[k, 0:1, :] + float(side * CAP)
            value = info[k, 1:2, :] if weighted else 1.0
            parts.append(jnp.where(slot == want, value, 0.0))
        return jnp.concatenate(parts, axis=1).astype(BF16)

    def tiles(n, body):
        def run(i, _):
            body(pl.ds(pl.multiple_of(i * COLS, COLS), COLS))
            return 0

        lax.fori_loop(0, n // COLS, run, 0)

    def dispatch(g):
        for k in sources[g]:
            if k:
                arrived(info.at[k], info_s.at[k], info_r.at[k], along_z(-k))
        pick = placing(g, False)

        def body(cols):
            got = jnp.dot(pick, x[g, :, cols], preferred_element_type=F32).astype(BF16)
            rows[g, 0:SLOT, cols] = got[0:SLOT]
            picked[g, :, cols] = got[SLOT:]

        tiles(2048, body)
        for k in (2, 3, 1):
            send(
                picked.at[g, pl.ds((k - 1) * SLOT, SLOT)], rows.at[g, pl.ds(k * SLOT, SLOT)],
                disp_s.at[g, k], disp_r.at[g, k], at_section(k),
            )

    def dispatched(g):
        for k in (1, 2, 3):
            arrived(
                rows.at[g, pl.ds(k * SLOT, SLOT)], disp_s.at[g, k], disp_r.at[g, k], at_section(-k)
            )

    def first(src, weight, dst, g, offset):
        def run(i, _):
            cols = pl.ds(pl.multiple_of(i * COLS, COLS), COLS)
            to = pl.ds(pl.multiple_of(offset + i * COLS, COLS), COLS)
            dst[g, :, to] = jax.nn.gelu(
                jnp.dot(src[g], weight[:, cols], preferred_element_type=F32), approximate=True
            ).astype(BF16)
            return 0

        lax.fori_loop(0, 512 // COLS, run, 0)

    def dense_second(g):
        def body(cols):
            dense[g, :, cols] = jnp.dot(
                hid[g, :, 0:512], own_out[:, cols], preferred_element_type=F32
            ) + jnp.dot(hid[g, :, 512:1024], far_out[:, cols], preferred_element_type=F32)

        tiles(2048, body)

    def expert_second(g):
        def body(cols):
            got = jnp.dot(ehid[g, :, 0:512], eown_out[:, cols], preferred_element_type=F32)
            got += jnp.dot(ehid[g, :, 512:1024], efar_out[:, cols], preferred_element_type=F32)
            got = got.astype(BF16)
            back[g, 0:SLOT, cols] = got[0:SLOT]
            leaving[g, :, cols] = got[SLOT:]

        tiles(2048, body)
        for k in (2, 3, 1):
            send(
                leaving.at[g, pl.ds((k - 1) * SLOT, SLOT)], back.at[g, pl.ds(k * SLOT, SLOT)],
                ret_s.at[g, k], ret_r.at[g, k], at_section(-k),
            )

    def combine(g):
        for k in (1, 2, 3):
            arrived(
                back.at[g, pl.ds(k * SLOT, SLOT)], ret_s.at[g, k], ret_r.at[g, k], at_section(k)
            )
        put = placing(g, True)

        def body(cols):
            dense[g, :, cols] += lax.dot_general(
                put, back[g, :, cols], (((0,), (0,)), ((), ())), preferred_element_type=F32
            )

        tiles(2048, body)

    for copy in local:
        copy.wait()
    leg2(0)
    leg2(1)
    hop_in(1)
    dispatch(0)
    first(x, own_in, hid, 0, 0)
    leg2(2)
    hop_in(2)
    dispatch(1)
    leg2(3)
    first(x, own_in, hid, 1, 0)
    dispatched(0)
    first(rows, eown_in, ehid, 0, 0)
    leg3(0)
    leg3(1)
    hop_in(3)
    dispatch(2)
    first(x, own_in, hid, 2, 0)
    dispatched(1)
    first(rows, eown_in, ehid, 1, 0)
    leg4(0)
    leg4(1)
    for i in range(2):
        half = mlp_half(i, core)
        send(half, half, core_s.at[i], core_r.at[i], other_core)
    hop_in(4)
    dispatch(3)
    first(x, own_in, hid, 3, 0)
    leg3(2)
    leg3(3)
    for i in range(2):
        arrived(mlp_half(i, 1 - core), core_s.at[i], core_r.at[i], other_core)
    for g in (3, 2, 1, 0):
        first(x, far_in, hid, g, 512)
        dense_second(g)
    dispatched(2)
    first(rows, eown_in, ehid, 2, 0)
    dispatched(3)
    first(rows, eown_in, ehid, 3, 0)
    leg4(2)
    leg4(3)
    for g in (3, 2, 1, 0):
        first(rows, efar_in, ehid, g, 512)
        expert_second(g)

    def passing(direction, hop, c):
        if hop == 4:
            return 3, pl.ds(ROWS + c * HALF, HALF)
        return hop - 1, pl.ds((1 - direction) * ROWS + c * HALF, HALF)

    combine(3)
    for hop in (4, 3, 2, 1):
        for i in range(1 if hop == 4 else 2):
            for direction in range(2):
                c = chunks(direction)[i]
                g, where = passing(direction, hop, c)
                mine = rs_out.at[direction, hop - 1, pl.ds(c * HALF, HALF)]
                total = dense[g, where, :]
                if hop < 3 or (hop == 3 and i == 0):
                    before = rs_in.at[direction, hop, pl.ds(c * HALF, HALF)]
                    arrived(
                        before, rs_s.at[direction, hop, c], rs_r.at[direction, hop, c],
                        along_z(-step[direction]),
                    )
                    total = total + before[...].astype(F32)
                mine[...] = total.astype(BF16)
                send(
                    mine, rs_in.at[direction, hop - 1, pl.ds(c * HALF, HALF)],
                    rs_s.at[direction, hop - 1, c], rs_r.at[direction, hop - 1, c],
                    along_z(step[direction]),
                )
        if hop > 1:
            combine(hop - 2)
    for c in range(2):
        part = pl.ds(c * HALF, HALF)
        total = dense[3, part, :]
        for direction in range(2):
            before = rs_in.at[direction, 0, part]
            arrived(
                before, rs_s.at[direction, 0, c], rs_r.at[direction, 0, c], along_z(-step[direction])
            )
            total = total + before[...].astype(F32)
        out_ref[part, :] = total.astype(BF16)

    for copy in sent:
        copy.wait_send()


def solution(mesh):
    def shards(inbound, expert_ids, gates, w_in, w_out, mlp_in, mlp_out):
        vmem, dma = pltpu.VMEM, pltpu.SemaphoreType.DMA
        return pl.pallas_call(
            relayed_experts,
            out_shape=jax.ShapeDtypeStruct((ROWS, 2048), BF16),
            in_specs=[pl.BlockSpec(memory_space=pltpu.VMEM)] * 2
            + [pl.BlockSpec(memory_space=pl.ANY)] * 5,
            out_specs=pl.BlockSpec(memory_space=pltpu.VMEM),
            scratch_shapes=[
                vmem((2048, 512), BF16), vmem((512, 2048), BF16),
                vmem((2048, 512), BF16), vmem((512, 2048), BF16),
                vmem((2048, 512), BF16), vmem((512, 2048), BF16),
                vmem((2048, 512), BF16), vmem((512, 2048), BF16),
                vmem((4, 2 * ROWS, 2048), BF16),
                vmem((8, 8, ROWS), F32),
                vmem((4, 3 * SLOT, 2048), BF16),
                vmem((4, 4 * SLOT, 2048), BF16),
                vmem((4, 2 * ROWS, 1024), BF16),
                vmem((4, 4 * SLOT, 1024), BF16),
                vmem((4, 2 * ROWS, 2048), F32),
                vmem((4, 3 * SLOT, 2048), BF16),
                vmem((4, 4 * SLOT, 2048), BF16),
                vmem((2, 4, ROWS, 2048), BF16),
                vmem((2, 4, ROWS, 2048), BF16),
                dma((4,)),
                dma((2,)), dma((2,)),
                dma((8,)), dma((8,)),
                dma((2, 4, 2)), dma((2, 4, 2)),
                dma((4,)), dma((4,)),
                dma((4, 4)), dma((4, 4)),
                dma((2,)), dma((2,)),
                dma((4, 4)), dma((4, 4)),
                dma((4, 4)), dma((4, 4)),
                dma((2, 4, 2)), dma((2, 4, 2)),
            ],
            compiler_params=pltpu.CompilerParams(
                collective_id=0, has_side_effects=True, vmem_limit_bytes=60 * 2**20
            ),
        )(
            expert_ids.reshape(1, ROWS), gates.reshape(1, ROWS), inbound,
            w_in[0], w_out[0], mlp_in, mlp_out,
        )

    return jax.shard_map(
        shards,
        mesh=mesh,
        in_specs=(
            P(("section", "dp", "expert"), None),
            P(("section", "dp", "expert"), None),
            P(("section", "dp", "expert"), None),
            P("section", None, "expert"),
            P("section", "expert", None),
            P(None, "expert"),
            P("expert", None),
        ),
        out_specs=P(("section", "dp", "expert"), None),
        check_vma=False,
    )
```

time: 724 us -> 163 us (0.23)
  waiting for transfers between devices: 648 us -> 0 us
  Pallas kernels: 0 us -> 160 us
  matrix products: 27.6 us -> 0 us
  blocking collectives: 25.1 us -> 0 us
  between operations: 13.2 us -> 0.01 us
    reduce_scatter x2 -> x0, waiting for transfers between devices: 410 us -> none  [the longest x1 211 us: shards(): lax.psum_scatter(jnp.dot(dense_hidden, mlp_out, preferred_element_type=jn...]
    all_gather x2 -> x0, waiting for transfers between devices: 232 us -> none  [the longest x1 127 us: shards(): lax.all_gather(tokens, 'expert', axis=0, tiled=True)]
    pallas_call x0 -> x1, Pallas kernels: none -> 160 us  [shards(): pl.pallas_call(relayed_experts, out_shape=jax.ShapeDtypeStruct((ROWS, 204...]
    dot_general x4 -> x0, matrix products: 27.6 us -> none  [the longest x1 14.4 us: shards(): jnp.dot(dense_hidden, mlp_out, preferred_element_type=jnp.float32)]
    all_to_all x2 -> x0, blocking collectives: 25.1 us -> none  [the longest x1 13.4 us: shards(): lax.all_to_all(leaving, 'section', split_axis=0, concat_axis=0, tiled=True)]
  transfers between devices with their start and end apart: 5 -> 0, of which waited for: 5 -> 0; matrix products, arithmetic and copies ran while one was open for 4% -> 0% of each run, Pallas kernels for 0% -> 0%
where the time goes in v1:
time: 163 us; the launch traced here: 162 us
  Pallas kernels  160 us (98%)
  local copies, waits for them, and re-layouts  1.88 us (1%)
    pallas_call x1, Pallas kernels, shards(): pl.pallas_call(relayed_experts, out_shape=jax.ShapeDtypeStruct((ROWS, 204...  160 us

profile of v1, /device:TPU:1, one launch (start us, length us, event | category | flops | bytes accessed | tf_op | source)
XLA Modules:
  0.0 162.0 jit_solution(15162607075377158972)
XLA Ops:
  0.0 160.1 %shard_map.73 = bf16[128,2048]{1,0:T(8,128)(2,1)} custom-call(s32[1,128]{1,0:T(1,128)} %bitcast.6, f32[1,128]{1,0:T(1,128)} %bitcast.7, bf16[128,2048]{1,0:T(8,128)(2,1)} %inbound.1, bf16[2048,512]{1,0:T(8,128)(2,1)} %bitcast.4, bf16[512,2048]{1,0:T(8,128)(2,1)} %bitcast.5, bf16[2048,512]{1,0:T(8,128)(2,1)} %mlp_in.1, bf16[512,2048]{1,0:T(8,128)(2,1)} %mlp_out.1), custom_call_target="tpu_custom_call" | custom-call | tf_op jit(solution)/shard_map/pallas_call | solution.py:363
  160.1 1.9 %copy.9 = bf16[128,2048]{1,0:T(8,128)(2,1)} copy(bf16[128,2048]{1,0:T(8,128)(2,1)} %shard_map.73) | data formatting | bytes 1048576

commit v2 on v1

v2 whole, which is shorter than its diff:
```python
import functools

import jax
import jax.numpy as jnp
from jax import lax
from jax.experimental import pallas as pl
from jax.experimental.pallas import tpu as pltpu
from jax.sharding import PartitionSpec as P

MESH = pl.DeviceIdType.MESH
F32 = jnp.float32
BF16 = jnp.bfloat16
ROWS = 128
HALF = 64
CAP = 20
BLOCKS = ((0, 1, 7), (2, 6), (3, 5), (4,))
TOKENS = tuple(len(group) * ROWS for group in BLOCKS)
TOKENS_AT = tuple(sum(TOKENS[:g]) for g in range(4))
SLOTS = (64, 48, 48, 32)
SLOTS_AT = tuple(4 * sum(SLOTS[:g]) for g in range(4))
PICKED_AT = tuple(3 * sum(SLOTS[:g]) for g in range(4))
BLOCK_AT = {k: TOKENS_AT[g] + i * ROWS for g in range(4) for i, k in enumerate(BLOCKS[g])}
COLS = 512


def relayed_experts(
    ids_ref, gates_ref, inbound, w_in, w_out, mlp_in, mlp_out, out_ref,
    own_in, own_out, far_in, far_out, eown_in, eown_out, efar_in, efar_out,
    x, info, picked, rows, hid, ehid, dense, leaving, back, rs_out, rs_in,
    local_sem, hand_s, hand_r, info_s, info_r, ag_s, ag_r, w1_s, w1_r, w2_s, w2_r,
    core_s, core_r, disp_s, disp_r, ret_s, ret_r, rs_s, rs_r,
):
    s, d, e = lax.axis_index("section"), lax.axis_index("dp"), lax.axis_index("expert")
    core = lax.rem(s, 2)
    flip_e = e + 1 - 2 * lax.rem(e, 2)

    def along_z(k):
        return (s, d, lax.rem(e + 2 * (k % 8), 16))

    def at_section(k):
        return (lax.rem(s + k % 4, 4), d, e)

    def along_x(k):
        return (s, lax.rem(d + k % 4, 4), e)

    other_core = (s + 1 - 2 * core, d, e)
    far_expert = (s, d, flip_e)
    far_mlp = (lax.rem(s + 2, 4), d, flip_e)

    barrier = pltpu.get_barrier_semaphore()
    partners = [along_z(k) for k in range(1, 8)] + [at_section(k) for k in (1, 2, 3)]
    partners += [along_x(1), along_x(3), far_expert, far_mlp]
    for partner in partners:
        pl.semaphore_signal(barrier, inc=1, device_id=partner, device_id_type=MESH)

    local = [
        pltpu.make_async_copy(src, dst, local_sem.at[i])
        for i, (src, dst) in enumerate(
            [(mlp_in, own_in), (mlp_out, own_out), (w_in, eown_in), (w_out, eown_out)]
        )
    ]
    for copy in local:
        copy.start()
    pl.semaphore_wait(barrier, len(partners))

    sent = []

    def send(src, dst, send_sem, recv_sem, device):
        copy = pltpu.make_async_remote_copy(
            src_ref=src, dst_ref=dst, send_sem=send_sem, recv_sem=recv_sem,
            device_id=device, device_id_type=MESH,
        )
        copy.start()
        sent.append(copy)

    def arrived(dst, send_sem, recv_sem, device):
        pltpu.make_async_remote_copy(
            src_ref=dst, dst_ref=dst, send_sem=send_sem, recv_sem=recv_sem,
            device_id=device, device_id_type=MESH,
        ).wait_recv()

    for c in range(2):
        part = pl.ds(c * HALF, HALF)
        send(inbound.at[part], x.at[part], hand_s.at[c], hand_r.at[c], at_section(1))

    streams = [
        (mlp_in, far_in, 256, core * 1024, far_mlp),
        None,
        (w_in, efar_in, 256, 0, far_expert),
        (w_out, efar_out, 64, 0, far_expert),
        (w_in, efar_in, 256, 1024, far_expert),
        (w_out, efar_out, 64, 256, far_expert),
    ]

    def quarter(i, ref, k, part=None):
        _, _, q, base, _ = streams[i]
        first = base + lax.rem(d + k % 4, 4) * q
        if part is None:
            return ref.at[pl.ds(pl.multiple_of(first, 64), q)]
        return ref.at[pl.ds(pl.multiple_of(first + part * (q // 2), 32), q // 2)]

    def leg1(i):
        src, dst, _, _, device = streams[i]
        send(quarter(i, src, 0), quarter(i, dst, 0), w1_s.at[i], w1_r.at[i], device)

    def leg2(i):
        dst, device = streams[i][1], streams[i][4]
        mine = quarter(i, dst, 0)
        arrived(mine, w1_s.at[i], w1_r.at[i], device)
        send(mine, mine, w2_s.at[i, 0], w2_r.at[i, 0], along_x(1))
        send(mine, mine, w2_s.at[i, 1], w2_r.at[i, 1], along_x(3))

    def leg3(i):
        dst = streams[i][1]
        arrived(quarter(i, dst, 3), w2_s.at[i, 0], w2_r.at[i, 0], along_x(3))
        part = quarter(i, dst, 3, 0)
        send(part, part, w2_s.at[i, 2], w2_r.at[i, 2], along_x(1))
        arrived(quarter(i, dst, 1), w2_s.at[i, 1], w2_r.at[i, 1], along_x(1))
        part = quarter(i, dst, 1, 1)
        send(part, part, w2_s.at[i, 3], w2_r.at[i, 3], along_x(3))

    def leg4(i):
        dst = streams[i][1]
        arrived(quarter(i, dst, 2, 0), w2_s.at[i, 2], w2_r.at[i, 2], along_x(3))
        arrived(quarter(i, dst, 2, 1), w2_s.at[i, 3], w2_r.at[i, 3], along_x(1))

    def mlp_half(i, ref, side):
        n = (1024, 256)[i]
        return ref.at[pl.ds(pl.multiple_of(side * n, 64), n)]

    def direct():
        src, dst = mlp_half(1, mlp_out, core), mlp_half(1, far_out, core)
        send(src, dst, w1_s.at[1], w1_r.at[1], far_mlp)

    def direct_in():
        arrived(mlp_half(1, far_out, core), w1_s.at[1], w1_r.at[1], far_mlp)

    def to_other_core(i):
        half = mlp_half(i, (far_in, far_out)[i], core)
        send(half, half, core_s.at[i], core_r.at[i], other_core)

    def from_other_core(i):
        arrived(mlp_half(i, (far_in, far_out)[i], 1 - core), core_s.at[i], core_r.at[i], other_core)

    leg1(0)

    ids = jnp.broadcast_to(ids_ref[...].astype(F32), (ROWS, ROWS))
    earlier = lax.broadcasted_iota(jnp.int32, (ROWS, ROWS), 0)
    token = lax.broadcasted_iota(jnp.int32, (ROWS, ROWS), 1)
    same = jnp.where((ids.T == ids) & (earlier < token), 1.0, 0.0)
    position = jnp.sum(same, axis=0, keepdims=True)
    relative = ids_ref[...] - s
    relative = jnp.where(relative < 0, relative + 4, relative).astype(F32)
    position = jnp.where(position < CAP, position, -1e6)
    line = lax.broadcasted_iota(jnp.int32, (8, ROWS), 0)
    info[0] = jnp.where(
        line == 0,
        jnp.broadcast_to(relative, (8, ROWS)),
        jnp.where(
            line == 1,
            jnp.broadcast_to(position, (8, ROWS)),
            jnp.broadcast_to(gates_ref[...], (8, ROWS)),
        ),
    )
    for k in range(1, 8):
        send(info.at[0], info.at[k], info_s.at[k], info_r.at[k], along_z(k))

    step = (1, -1)

    def block(direction, hop):
        return BLOCK_AT[hop if direction == 0 else 8 - hop]

    def place(direction, hop, c):
        return x.at[pl.ds(block(direction, hop) + c * HALF, HALF)]

    def chunks(direction):
        return (0, 1) if direction == 0 else (1, 0)

    def hop_out(direction, hop, c, src):
        send(
            src, place(direction, hop, c),
            ag_s.at[direction, hop - 1, c], ag_r.at[direction, hop - 1, c],
            along_z(step[direction]),
        )

    def hop_in(hop, i):
        for direction in range(2):
            c = chunks(direction)[i]
            dst = place(direction, hop, c)
            arrived(
                dst, ag_s.at[direction, hop - 1, c], ag_r.at[direction, hop - 1, c],
                along_z(-step[direction]),
            )
            if hop < 3 or (hop == 3 and i == 0):
                hop_out(direction, hop + 1, c, dst)

    for c in range(2):
        own = x.at[pl.ds(c * HALF, HALF)]
        arrived(own, hand_s.at[c], hand_r.at[c], at_section(3))
        for direction in range(2):
            hop_out(direction, 1, c, own)
        leg1((2, 4)[c])

    def placing(g):
        parts = []
        for side, k in enumerate(BLOCKS[g]):
            slot = lax.broadcasted_iota(jnp.int32, (4 * SLOTS[g], ROWS), 0).astype(F32)
            want = info[k, 0:1, :] * float(SLOTS[g]) + info[k, 1:2, :] + float(side * CAP)
            parts.append(jnp.where(slot == want, 1.0, 0.0))
        return jnp.concatenate(parts, axis=1).astype(BF16)

    def weighting(g):
        parts = []
        for side, k in enumerate(BLOCKS[g]):
            columns = info[k].T
            slot = lax.broadcasted_iota(jnp.int32, (ROWS, 4 * SLOTS[g]), 1).astype(F32)
            want = columns[:, 0:1] * float(SLOTS[g]) + columns[:, 1:2] + float(side * CAP)
            parts.append(jnp.where(slot == want, columns[:, 2:3], 0.0))
        return jnp.concatenate(parts, axis=0).astype(BF16)

    def of_group(g):
        return pl.ds(TOKENS_AT[g], TOKENS[g])

    def slots_of(g):
        return pl.ds(SLOTS_AT[g], 4 * SLOTS[g])

    def slot_rows(g, k):
        return pl.ds(SLOTS_AT[g] + k * SLOTS[g], SLOTS[g])

    def picked_rows(g, k):
        return pl.ds(PICKED_AT[g] + (k - 1) * SLOTS[g], SLOTS[g])

    def tiles(n, body):
        def run(i, _):
            body(pl.ds(pl.multiple_of(i * COLS, COLS), COLS))
            return 0

        lax.fori_loop(0, n // COLS, run, 0)

    def dispatch(g):
        for k in BLOCKS[g]:
            if k:
                arrived(info.at[k], info_s.at[k], info_r.at[k], along_z(-k))
        pick = placing(g)

        def body(cols):
            got = jnp.dot(pick, x[of_group(g), cols], preferred_element_type=F32).astype(BF16)
            rows[slot_rows(g, 0), cols] = got[0 : SLOTS[g]]
            picked[pl.ds(PICKED_AT[g], 3 * SLOTS[g]), cols] = got[SLOTS[g] :]

        tiles(2048, body)
        for k in (2, 3, 1):
            send(
                picked.at[picked_rows(g, k)], rows.at[slot_rows(g, k)],
                disp_s.at[g, k], disp_r.at[g, k], at_section(k),
            )

    def dispatched(g):
        for k in (1, 2, 3):
            arrived(rows.at[slot_rows(g, k)], disp_s.at[g, k], disp_r.at[g, k], at_section(-k))

    def first(src, weight, dst, where, offset):
        dst[where, offset : offset + 512] = jax.nn.gelu(
            jnp.dot(src[where, :], weight[...], preferred_element_type=F32), approximate=True
        ).astype(BF16)

    def dense_near_first(g):
        first(x, own_in, hid, of_group(g), 0)

    def dense_far_first(g):
        first(x, far_in, hid, of_group(g), 512)

    def expert_near_first(g):
        first(rows, eown_in, ehid, slots_of(g), 0)

    def expert_far_first(g):
        first(rows, efar_in, ehid, slots_of(g), 512)

    def dense_near(g):
        def body(cols):
            dense[of_group(g), cols] = jnp.dot(
                hid[of_group(g), 0:512], own_out[:, cols], preferred_element_type=F32
            )

        tiles(2048, body)

    def dense_far(g):
        def body(cols):
            dense[of_group(g), cols] += jnp.dot(
                hid[of_group(g), 512:1024], far_out[:, cols], preferred_element_type=F32
            )

        tiles(2048, body)

    def expert_second(g):
        def body(cols):
            near, far = ehid[slots_of(g), 0:512], ehid[slots_of(g), 512:1024]
            got = jnp.dot(near, eown_out[:, cols], preferred_element_type=F32)
            got += jnp.dot(far, efar_out[:, cols], preferred_element_type=F32)
            got = got.astype(BF16)
            back[slot_rows(g, 0), cols] = got[0 : SLOTS[g]]
            leaving[pl.ds(PICKED_AT[g], 3 * SLOTS[g]), cols] = got[SLOTS[g] :]

        tiles(2048, body)

    def give_back(g):
        for k in (2, 3, 1):
            send(
                leaving.at[picked_rows(g, k)], back.at[slot_rows(g, k)],
                ret_s.at[g, k], ret_r.at[g, k], at_section(-k),
            )

    def combine(g):
        for k in (1, 2, 3):
            arrived(back.at[slot_rows(g, k)], ret_s.at[g, k], ret_r.at[g, k], at_section(k))
        put = weighting(g)

        def body(cols):
            dense[of_group(g), cols] += jnp.dot(
                put, back[slots_of(g), cols], preferred_element_type=F32
            )

        tiles(2048, body)

    leg2(0)
    for copy in local:
        copy.wait()
    hop_in(1, 0)
    leg2(2)
    leg1(3)
    hop_in(1, 1)
    leg2(4)
    leg1(5)
    dense_near_first(0)
    leg3(2)
    hop_in(2, 0)
    dispatch(0)
    leg2(3)
    leg3(4)
    hop_in(2, 1)
    leg2(5)
    direct()
    dispatch(1)
    dense_near(0)
    leg4(2)
    hop_in(3, 0)
    leg3(3)
    leg4(4)
    dense_near_first(1)
    hop_in(3, 1)
    dispatch(2)
    leg3(5)
    leg3(0)
    dense_near_first(2)
    hop_in(4, 0)
    dispatch(3)
    dense_near(2)
    leg4(3)
    dense_near_first(3)
    dense_near(1)
    dispatched(2)
    expert_near_first(2)
    expert_far_first(2)
    leg4(5)
    expert_second(2)
    give_back(2)
    leg4(0)
    to_other_core(0)
    direct_in()
    to_other_core(1)
    dispatched(3)
    expert_near_first(3)
    expert_far_first(3)
    expert_second(3)
    from_other_core(0)
    dense_far_first(2)
    from_other_core(1)
    dense_far(2)
    dense_far_first(3)
    dense_near(3)
    dense_far(3)

    def passing(direction, hop, c):
        return pl.ds(block(1 - direction, hop) + c * HALF, HALF)

    def hop_back(hop, i):
        for direction in range(2):
            c = chunks(direction)[i]
            mine = rs_out.at[direction, hop - 1, pl.ds(c * HALF, HALF)]
            total = dense[passing(direction, hop, c), :]
            if hop < 3 or (hop == 3 and i == 0):
                before = rs_in.at[direction, hop, pl.ds(c * HALF, HALF)]
                arrived(
                    before, rs_s.at[direction, hop, c], rs_r.at[direction, hop, c],
                    along_z(-step[direction]),
                )
                total = total + before[...].astype(F32)
            mine[...] = total.astype(BF16)
            send(
                mine, rs_in.at[direction, hop - 1, pl.ds(c * HALF, HALF)],
                rs_s.at[direction, hop - 1, c], rs_r.at[direction, hop - 1, c],
                along_z(step[direction]),
            )

    combine(2)
    give_back(3)
    hop_back(3, 1)
    dispatched(1)
    expert_near_first(1)
    expert_far_first(1)
    expert_second(1)
    combine(3)
    give_back(1)
    hop_back(4, 0)
    dispatched(0)
    expert_near_first(0)
    expert_far_first(0)
    expert_second(0)
    dense_far_first(1)
    dense_far(1)
    hop_back(3, 0)
    combine(1)
    give_back(0)
    hop_back(2, 1)
    dense_far_first(0)
    hop_back(2, 0)
    dense_far(0)
    combine(0)
    hop_back(1, 1)
    hop_back(1, 0)
    for c in range(2):
        part = pl.ds(c * HALF, HALF)
        total = dense[part, :]
        for direction in (c, 1 - c):
            before = rs_in.at[direction, 0, part]
            arrived(
                before, rs_s.at[direction, 0, c], rs_r.at[direction, 0, c], along_z(-step[direction])
            )
            total = total + before[...].astype(F32)
        out_ref[part, :] = total.astype(BF16)

    for copy in sent:
        copy.wait_send()


def solution(mesh):
    def shards(inbound, expert_ids, gates, w_in, w_out, mlp_in, mlp_out):
        vmem, dma = pltpu.VMEM, pltpu.SemaphoreType.DMA
        return pl.pallas_call(
            relayed_experts,
            out_shape=jax.ShapeDtypeStruct((ROWS, 2048), BF16),
            in_specs=[pl.BlockSpec(memory_space=pltpu.VMEM)] * 2
            + [pl.BlockSpec(memory_space=pl.ANY)] * 5,
            out_specs=pl.BlockSpec(memory_space=pltpu.VMEM),
            scratch_shapes=[
                vmem((2048, 512), BF16), vmem((512, 2048), BF16),
                vmem((2048, 512), BF16), vmem((512, 2048), BF16),
                vmem((2048, 512), BF16), vmem((512, 2048), BF16),
                vmem((2048, 512), BF16), vmem((512, 2048), BF16),
                vmem((8 * ROWS, 2048), BF16),
                vmem((8, 8, ROWS), F32),
                vmem((3 * sum(SLOTS), 2048), BF16),
                vmem((4 * sum(SLOTS), 2048), BF16),
                vmem((8 * ROWS, 1024), BF16),
                vmem((4 * sum(SLOTS), 1024), BF16),
                vmem((8 * ROWS, 2048), F32),
                vmem((3 * sum(SLOTS), 2048), BF16),
                vmem((4 * sum(SLOTS), 2048), BF16),
                vmem((2, 4, ROWS, 2048), BF16),
                vmem((2, 4, ROWS, 2048), BF16),
                dma((4,)),
                dma((2,)), dma((2,)),
                dma((8,)), dma((8,)),
                dma((2, 4, 2)), dma((2, 4, 2)),
                dma((6,)), dma((6,)),
                dma((6, 4)), dma((6, 4)),
                dma((2,)), dma((2,)),
                dma((4, 4)), dma((4, 4)),
                dma((4, 4)), dma((4, 4)),
                dma((2, 4, 2)), dma((2, 4, 2)),
            ],
            compiler_params=pltpu.CompilerParams(
                collective_id=0, has_side_effects=True, vmem_limit_bytes=60 * 2**20
            ),
        )(
            expert_ids.reshape(1, ROWS), gates.reshape(1, ROWS), inbound,
            w_in[0], w_out[0], mlp_in, mlp_out,
        )

    return jax.shard_map(
        shards,
        mesh=mesh,
        in_specs=(
            P(("section", "dp", "expert"), None),
            P(("section", "dp", "expert"), None),
            P(("section", "dp", "expert"), None),
            P("section", None, "expert"),
            P("section", "expert", None),
            P(None, "expert"),
            P("expert", None),
        ),
        out_specs=P(("section", "dp", "expert"), None),
        check_vma=False,
    )
```

time: 163 us -> 136 us (0.83)
  Pallas kernels: 160 us -> 134 us
    pallas_call x1, Pallas kernels: 160 us -> 134 us  [shards(): pl.pallas_call(relayed_experts, out_shape=jax.ShapeDtypeStruct((ROWS, 204...]
where the time goes in v2:
time: 136 us
  Pallas kernels  134 us (99%)
  local copies, waits for them, and re-layouts  1.88 us (1%)
    pallas_call x1, Pallas kernels, shards(): pl.pallas_call(relayed_experts, out_shape=jax.ShapeDtypeStruct((ROWS, 204...  134 us

profile of v2, /device:TPU:1, one launch (start us, length us, event | category | flops | bytes accessed | tf_op | source)
XLA Modules:
  0.0 135.8 jit_solution(12510678744554168923)
XLA Ops:
  0.0 133.9 %shard_map.73 = bf16[128,2048]{1,0:T(8,128)(2,1)} custom-call(s32[1,128]{1,0:T(1,128)} %bitcast.6, f32[1,128]{1,0:T(1,128)} %bitcast.7, bf16[128,2048]{1,0:T(8,128)(2,1)} %inbound.1, bf16[2048,512]{1,0:T(8,128)(2,1)} %bitcast.4, bf16[512,2048]{1,0:T(8,128)(2,1)} %bitcast.5, bf16[2048,512]{1,0:T(8,128)(2,1)} %mlp_in.1, bf16[512,2048]{1,0:T(8,128)(2,1)} %mlp_out.1), custom_call_target="tpu_custom_call" | custom-call | tf_op jit(solution)/shard_map/pallas_call | solution.py:449
  133.9 1.9 %copy.9 = bf16[128,2048]{1,0:T(8,128)(2,1)} copy(bf16[128,2048]{1,0:T(8,128)(2,1)} %shard_map.73) | data formatting | bytes 1048576

commit v3 on v2

--- a/solution.py
+++ b/solution.py
@@ -19,6 +19,7 @@
 SLOTS = (64, 48, 48, 32)
 SLOTS_AT = tuple(4 * sum(SLOTS[:g]) for g in range(4))
 PICKED_AT = tuple(3 * sum(SLOTS[:g]) for g in range(4))
+FAR_SIDE = (1,)
 BLOCK_AT = {k: TOKENS_AT[g] + i * ROWS for g in range(4) for i, k in enumerate(BLOCKS[g])}
 COLS = 512
 
@@ -40,6 +41,12 @@
     def at_section(k):
         return (lax.rem(s + k % 4, 4), d, e)
 
+    def peer(g, k):
+        t, _, _ = at_section(k)
+        if g in FAR_SIDE:
+            return (t, d, jnp.where(t // 2 == s // 2, e, flip_e))
+        return (t, d, e)
+
     def along_x(k):
         return (s, lax.rem(d + k % 4, 4), e)
 
@@ -49,7 +56,7 @@
 
     barrier = pltpu.get_barrier_semaphore()
     partners = [along_z(k) for k in range(1, 8)] + [at_section(k) for k in (1, 2, 3)]
-    partners += [along_x(1), along_x(3), far_expert, far_mlp]
+    partners += [(lax.rem(s + 3 - 2 * core, 4), d, flip_e), along_x(1), along_x(3), far_expert, far_mlp]
     for partner in partners:
         pl.semaphore_signal(barrier, inc=1, device_id=partner, device_id_type=MESH)
 
@@ -84,7 +91,7 @@
         send(inbound.at[part], x.at[part], hand_s.at[c], hand_r.at[c], at_section(1))
 
     streams = [
-        (mlp_in, far_in, 256, core * 1024, far_mlp),
+        (mlp_out, far_out, 64, core * 256, far_mlp),
         None,
         (w_in, efar_in, 256, 0, far_expert),
         (w_out, efar_out, 64, 0, far_expert),
@@ -129,11 +136,11 @@
         return ref.at[pl.ds(pl.multiple_of(side * n, 64), n)]
 
     def direct():
-        src, dst = mlp_half(1, mlp_out, core), mlp_half(1, far_out, core)
+        src, dst = mlp_half(0, mlp_in, core), mlp_half(0, far_in, core)
         send(src, dst, w1_s.at[1], w1_r.at[1], far_mlp)
 
     def direct_in():
-        arrived(mlp_half(1, far_out, core), w1_s.at[1], w1_r.at[1], far_mlp)
+        arrived(mlp_half(0, far_in, core), w1_s.at[1], w1_r.at[1], far_mlp)
 
     def to_other_core(i):
         half = mlp_half(i, (far_in, far_out)[i], core)
@@ -252,12 +259,12 @@
         for k in (2, 3, 1):
             send(
                 picked.at[picked_rows(g, k)], rows.at[slot_rows(g, k)],
-                disp_s.at[g, k], disp_r.at[g, k], at_section(k),
+                disp_s.at[g, k], disp_r.at[g, k], peer(g, k),
             )
 
     def dispatched(g):
         for k in (1, 2, 3):
-            arrived(rows.at[slot_rows(g, k)], disp_s.at[g, k], disp_r.at[g, k], at_section(-k))
+            arrived(rows.at[slot_rows(g, k)], disp_s.at[g, k], disp_r.at[g, k], peer(g, -k))
 
     def first(src, weight, dst, where, offset):
         dst[where, offset : offset + 512] = jax.nn.gelu(
@@ -307,12 +314,12 @@
         for k in (2, 3, 1):
             send(
                 leaving.at[picked_rows(g, k)], back.at[slot_rows(g, k)],
-                ret_s.at[g, k], ret_r.at[g, k], at_section(-k),
+                ret_s.at[g, k], ret_r.at[g, k], peer(g, -k),
             )
 
     def combine(g):
         for k in (1, 2, 3):
-            arrived(back.at[slot_rows(g, k)], ret_s.at[g, k], ret_r.at[g, k], at_section(k))
+            arrived(back.at[slot_rows(g, k)], ret_s.at[g, k], ret_r.at[g, k], peer(g, k))
         put = weighting(g)
 
         def body(cols):
@@ -322,7 +329,6 @@
 
         tiles(2048, body)
 
-    leg2(0)
     for copy in local:
         copy.wait()
     hop_in(1, 0)
@@ -334,39 +340,37 @@
     dense_near_first(0)
     leg3(2)
     hop_in(2, 0)
-    dispatch(0)
     leg2(3)
     leg3(4)
     hop_in(2, 1)
     leg2(5)
+    leg2(0)
     direct()
-    dispatch(1)
-    dense_near(0)
+    dispatch(0)
     leg4(2)
     hop_in(3, 0)
     leg3(3)
     leg4(4)
-    dense_near_first(1)
+    dense_near(0)
     hop_in(3, 1)
     dispatch(2)
     leg3(5)
-    leg3(0)
     dense_near_first(2)
     hop_in(4, 0)
     dispatch(3)
+    leg4(3)
     dense_near(2)
-    leg4(3)
-    dense_near_first(3)
-    dense_near(1)
     dispatched(2)
     expert_near_first(2)
     expert_far_first(2)
     leg4(5)
+    leg3(0)
     expert_second(2)
     give_back(2)
+    direct_in()
+    to_other_core(0)
+    dispatch(1)
     leg4(0)
-    to_other_core(0)
-    direct_in()
     to_other_core(1)
     dispatched(3)
     expert_near_first(3)
@@ -374,11 +378,9 @@
     expert_second(3)
     from_other_core(0)
     dense_far_first(2)
+    dense_near_first(3)
     from_other_core(1)
     dense_far(2)
-    dense_far_first(3)
-    dense_near(3)
-    dense_far(3)
 
     def passing(direction, hop, c):
         return pl.ds(block(1 - direction, hop) + c * HALF, HALF)
@@ -405,22 +407,27 @@
     combine(2)
     give_back(3)
     hop_back(3, 1)
+    dense_far_first(3)
+    dense_near(3)
+    dense_far(3)
     dispatched(1)
     expert_near_first(1)
     expert_far_first(1)
     expert_second(1)
+    give_back(1)
     combine(3)
-    give_back(1)
     hop_back(4, 0)
     dispatched(0)
     expert_near_first(0)
     expert_far_first(0)
     expert_second(0)
+    give_back(0)
+    dense_near_first(1)
+    dense_near(1)
     dense_far_first(1)
     dense_far(1)
     hop_back(3, 0)
     combine(1)
-    give_back(0)
     hop_back(2, 1)
     dense_far_first(0)
     hop_back(2, 0)

time: 136 us -> 129 us (0.949)
  Pallas kernels: 134 us -> 127 us
    pallas_call x1, Pallas kernels: 134 us -> 127 us  [shards(): pl.pallas_call(relayed_experts, out_shape=jax.ShapeDtypeStruct((ROWS, 204...]
where the time goes in v3:
time: 129 us
  Pallas kernels  127 us (98%)
  local copies, waits for them, and re-layouts  1.88 us (1%)
    pallas_call x1, Pallas kernels, shards(): pl.pallas_call(relayed_experts, out_shape=jax.ShapeDtypeStruct((ROWS, 204...  127 us

profile of v3, /device:TPU:1, one launch (start us, length us, event | category | flops | bytes accessed | tf_op | source)
XLA Modules:
  0.0 129.2 jit_solution(7441231153636229175)
XLA Ops:
  0.0 127.3 %shard_map.73 = bf16[128,2048]{1,0:T(8,128)(2,1)} custom-call(s32[1,128]{1,0:T(1,128)} %bitcast.6, f32[1,128]{1,0:T(1,128)} %bitcast.7, bf16[128,2048]{1,0:T(8,128)(2,1)} %inbound.1, bf16[2048,512]{1,0:T(8,128)(2,1)} %bitcast.4, bf16[512,2048]{1,0:T(8,128)(2,1)} %bitcast.5, bf16[2048,512]{1,0:T(8,128)(2,1)} %mlp_in.1, bf16[512,2048]{1,0:T(8,128)(2,1)} %mlp_out.1), custom_call_target="tpu_custom_call" | custom-call | tf_op jit(solution)/shard_map/pallas_call | solution.py:456
  127.3 1.9 %copy.9 = bf16[128,2048]{1,0:T(8,128)(2,1)} copy(bf16[128,2048]{1,0:T(8,128)(2,1)} %shard_map.73) | data formatting | bytes 1048576

commit v4 on v3

--- a/solution.py
+++ b/solution.py
@@ -21,7 +21,7 @@
 PICKED_AT = tuple(3 * sum(SLOTS[:g]) for g in range(4))
 FAR_SIDE = (1,)
 BLOCK_AT = {k: TOKENS_AT[g] + i * ROWS for g in range(4) for i, k in enumerate(BLOCKS[g])}
-COLS = 512
+COLS = 1024
 
 
 def relayed_experts(
@@ -337,6 +337,7 @@
     hop_in(1, 1)
     leg2(4)
     leg1(5)
+    direct()
     dense_near_first(0)
     leg3(2)
     hop_in(2, 0)
@@ -345,7 +346,6 @@
     hop_in(2, 1)
     leg2(5)
     leg2(0)
-    direct()
     dispatch(0)
     leg4(2)
     hop_in(3, 0)

time: 129 us -> 128 us (level)
  no operation moved by 1% of the time
where the time goes in v4:
time: 128 us
  Pallas kernels  126 us (98%)
  local copies, waits for them, and re-layouts  1.88 us (1%)
    pallas_call x1, Pallas kernels, shards(): pl.pallas_call(relayed_experts, out_shape=jax.ShapeDtypeStruct((ROWS, 204...  126 us

profile of v4, /device:TPU:1, one launch (start us, length us, event | category | flops | bytes accessed | tf_op | source)
XLA Modules:
  0.0 128.3 jit_solution(8341285072295235633)
XLA Ops:
  0.0 126.4 %shard_map.73 = bf16[128,2048]{1,0:T(8,128)(2,1)} custom-call(s32[1,128]{1,0:T(1,128)} %bitcast.6, f32[1,128]{1,0:T(1,128)} %bitcast.7, bf16[128,2048]{1,0:T(8,128)(2,1)} %inbound.1, bf16[2048,512]{1,0:T(8,128)(2,1)} %bitcast.4, bf16[512,2048]{1,0:T(8,128)(2,1)} %bitcast.5, bf16[2048,512]{1,0:T(8,128)(2,1)} %mlp_in.1, bf16[512,2048]{1,0:T(8,128)(2,1)} %mlp_out.1), custom_call_target="tpu_custom_call" | custom-call | tf_op jit(solution)/shard_map/pallas_call | solution.py:456
  126.4 1.9 %copy.9 = bf16[128,2048]{1,0:T(8,128)(2,1)} copy(bf16[128,2048]{1,0:T(8,128)(2,1)} %shard_map.73) | data formatting | bytes 1048576
